TPU v7x, 32 devices: a whole 2x2x4 slice. The times are simulated.
32 devices in a mesh: blk: 8 (over z, core), rep: 4 (over y, x).
Axes of the slice: x: 2, y: 2, z: 4, core: 2. Of those that a mesh axis runs over, the one named last changes fastest.
Arguments:
- features: bfloat16 [32768, 256], P('blk'), may hold values from -6 to 6
- state: bfloat16 [32768, 256], P('blk'), may hold values from -1 to 1
- tiles: bfloat16 [8, 8, 64, 128, 128], P('blk', 'rep'), may hold values from -0.25 to 0.25
- tile_count: int32 [8, 8], P('blk', 'rep'), may hold values from 0 to 64, as said below
- tile_rows: int32 [8, 8, 64], P('blk', 'rep'), may hold values from 0 to 31, as said below
- tile_cols: int32 [8, 8, 64], P('blk', 'rep'), may hold values from 0 to 31, as said below
- w_graph: bfloat16 [256, 256], replicated, may hold values from -0.375 to 0.375
- b_graph: float32 [256], replicated, may hold values from -1 to 1
- w_input: bfloat16 [256, 768], replicated, may hold values from -0.375 to 0.375
- w_state: bfloat16 [256, 512], replicated, may hold values from -0.375 to 0.375
- w_cand: bfloat16 [256, 256], replicated, may hold values from -0.375 to 0.375
- b_gates: float32 [768], replicated, may hold values from -1 to 1
- cotangent: bfloat16 [32768, 256], P('blk'), may hold values from -6 to 6
Outputs:
- new_state: bfloat16 [32768, 256], P('blk')
- state_grad: bfloat16 [32768, 256], P('blk')
- grad_graph: float32 [256, 256], replicated
- grad_graph_bias: float32 [256], replicated
- grad_input: float32 [256, 768], replicated
- grad_state: float32 [256, 512], replicated
- grad_cand: float32 [256, 256], replicated
- grad_gates: float32 [768], replicated
Inputs may be any that keep to these rules, and one draw needn't show every extreme that they name: Only the first tile_count[b, s] entries of a section list are used; some list holds exactly 64 tiles in every draw, and some lists are empty. `tile_rows`: row tile of a list entry; the (row, column) positions within one list are distinct. `tile_cols`: column tile of a list entry within its section's block of nodes.
All inputs are finite; a program needn't handle non-finite values.
Results may differ from a plain program's by a relative error of at most 0.02.
Values may be sent and summed in bfloat16 or wider, within the bound.
A program may use at most 128 MiB of HBM per device.

v0:
```python
import jax
import jax.numpy as jnp
from jax import lax
from jax.sharding import PartitionSpec as P


def from_root(block, axis, owner):
    block = jnp.where(lax.axis_index(axis) == owner, block, jnp.zeros_like(block))
    return lax.psum(block, axis)


def contract_first(left, right):
    return lax.dot_general(
        left, right, (((0,), (0,)), ((), ())), preferred_element_type=jnp.float32
    )


def contract_last(left, right):
    return lax.dot_general(
        left, right, (((1,), (1,)), ((), ())), preferred_element_type=jnp.float32
    )


def cell_step(summed, state, cotangent, w_graph, b_graph, w_input, w_state, w_cand, b_gates):
    width = w_cand.shape[0]
    summed_b = summed.astype(jnp.bfloat16)
    preact = jnp.dot(summed_b, w_graph, preferred_element_type=jnp.float32) + b_graph
    graph_out = jnp.tanh(preact)
    graph_b = graph_out.astype(jnp.bfloat16)
    from_input = jnp.dot(graph_b, w_input, preferred_element_type=jnp.float32) + b_gates
    from_state = jnp.dot(state, w_state, preferred_element_type=jnp.float32)
    reset_gate = jax.nn.sigmoid(from_input[:, :width] + from_state[:, :width])
    update_gate = jax.nn.sigmoid(from_input[:, width : 2 * width] + from_state[:, width:])
    state_f = state.astype(jnp.float32)
    reset_state = (reset_gate * state_f).astype(jnp.bfloat16)
    candidate = jnp.tanh(
        from_input[:, 2 * width :]
        + jnp.dot(reset_state, w_cand, preferred_element_type=jnp.float32)
    )
    new_state = update_gate * state_f + (1.0 - update_gate) * candidate
    upstream = cotangent.astype(jnp.float32)
    grad_update = upstream * (state_f - candidate) * update_gate * (1.0 - update_gate)
    grad_cand_f = upstream * (1.0 - update_gate) * (1.0 - candidate * candidate)
    grad_cand_b = grad_cand_f.astype(jnp.bfloat16)
    grad_reset_state = contract_last(grad_cand_b, w_cand)
    grad_reset = grad_reset_state * state_f * reset_gate * (1.0 - reset_gate)
    gate_grads = jnp.concatenate(
        [grad_reset.astype(jnp.bfloat16), grad_update.astype(jnp.bfloat16), grad_cand_b], axis=1
    )
    gate_sums = jnp.concatenate(
        [jnp.sum(grad_reset, axis=0), jnp.sum(grad_update, axis=0), jnp.sum(grad_cand_f, axis=0)]
    )
    grad_input = contract_first(graph_b, gate_grads)
    grad_state = contract_first(state, gate_grads[:, : 2 * width])
    grad_cand = contract_first(reset_state, grad_cand_b)
    grad_graph_out = contract_last(gate_grads, w_input)
    grad_preact = grad_graph_out * (1.0 - graph_out * graph_out)
    grad_graph = contract_first(summed_b, grad_preact.astype(jnp.bfloat16))
    graph_bias_sum = jnp.sum(grad_preact, axis=0)
    state_grad = (
        upstream * update_gate
        + grad_reset_state * reset_gate
        + contract_last(gate_grads[:, : 2 * width], w_state)
    )
    return (
        new_state.astype(jnp.bfloat16),
        state_grad.astype(jnp.bfloat16),
        (grad_graph, graph_bias_sum, grad_input, grad_state, grad_cand, gate_sums),
    )


def local(
    features,
    state,
    tiles,
    tile_count,
    tile_rows,
    tile_cols,
    w_graph,
    b_graph,
    w_input,
    w_state,
    w_cand,
    b_gates,
    cotangent,
):
    per_rep = tiles.shape[1]
    list_cap = tiles.shape[2]
    tile_side = tiles.shape[3]
    row_count = features.shape[0]
    feat_width = features.shape[1]
    row_tiles = row_count // tile_side
    rep_index = lax.axis_index("rep")
    scale = float(row_count * lax.axis_size("blk")) ** (-0.5)
    entry_ids = jnp.arange(list_cap, dtype=jnp.int32)
    row_ids = jnp.arange(row_tiles, dtype=jnp.int32)
    partial_value = jnp.zeros((row_tiles, tile_side, feat_width), jnp.float32)
    for slot in range(per_rep):
        owner = rep_index * per_rep + slot
        section_feat = from_root(features, "blk", owner)
        section_tiles = section_feat.reshape(row_tiles, tile_side, feat_width)
        picked = jnp.take(section_tiles, tile_cols[0, slot], axis=0)
        products = jnp.einsum(
            "mab,mbf->maf", tiles[0, slot], picked, preferred_element_type=jnp.float32
        )
        in_list = entry_ids < tile_count[0, slot]
        placing = ((tile_rows[0, slot][None, :] == row_ids[:, None]) & in_list[None, :]).astype(
            jnp.float32
        )
        partial_value = partial_value + jnp.einsum("rm,maf->raf", placing, products)
    flat = partial_value.reshape(row_count, feat_width)
    totals = lax.psum(flat, "rep")
    new_state, state_grad, grads = cell_step(
        totals, state, cotangent, w_graph, b_graph, w_input, w_state, w_cand, b_gates
    )
    grad_graph, graph_bias_sum, grad_input, grad_state, grad_cand, gate_sums = grads
    summed_grads = lax.psum(
        (
            grad_graph * scale,
            graph_bias_sum * scale,
            grad_input * scale,
            grad_state * scale,
            grad_cand * scale,
            gate_sums * scale,
        ),
        "blk",
    )
    return (
        new_state,
        state_grad,
        summed_grads[0],
        summed_grads[1],
        summed_grads[2],
        summed_grads[3],
        summed_grads[4],
        summed_grads[5],
    )


def solution(mesh):
    in_specs = (
        P("blk", None),
        P("blk", None),
        P("blk", "rep", None, None, None),
        P("blk", "rep"),
        P("blk", "rep", None),
        P("blk", "rep", None),
        P(),
        P(),
        P(),
        P(),
        P(),
        P(),
        P("blk", None),
    )
    out_specs = (P("blk", None), P("blk", None), P(), P(), P(), P(), P(), P())
    return jax.shard_map(local, mesh=mesh, in_specs=in_specs, out_specs=out_specs, check_vma=False)
```

profile of v0, /device:TPU:0, one launch (start us, length us, event | category | flops | bytes accessed | tf_op | source)
XLA Modules:
  0.0 422.5 jit_solution(1578624425330768897)
XLA Ops:
  7.2 0.0 copy-start
  7.2 0.0 all-reduce.9.cloned.1.call-start
  7.2 0.0 copy-start.16
  7.2 0.0 copy-start.17
  7.3 0.0 copy-start.18
  7.3 0.0 copy-start.3
  7.3 0.0 copy-start.11
  7.3 4.0 broadcast_select_fusion.1
  11.3 0.0 all-reduce.9.cloned.1.call-update
  11.3 0.0 all-reduce.7.cloned.1.call-start
  11.4 0.0 copy-done.16
  11.4 0.6 fusion.78
  12.0 0.6 iota_compare_fusion.3
  12.6 0.7 iota_compare_fusion.2
  13.3 0.0 copy-done.17
  13.3 0.0 copy-done.18
  13.4 0.0 copy-done.3
  13.4 0.0 copy-done.11
  13.4 4.5 %fusion.80 = f32[4096,512]{1,0:T(8,128)} fusion(bf16[4096,256]{1,0:T(8,128)(2,1)S(1)} %copy-done.3, bf16[256,512]{1,0:T(8,128)(2,1)S(1)} %copy-done.11), kind=kOutput, calls=%fused_computation.106 | convolution fusion | flops 1073741824 | bytes 10747904 | tf_op jit(solution)/shard_map/dot_general | solution.py:31
  17.8 93.3 %all-reduce.9.cloned.1.call-done = (bf16[32,128,256]{2,1,0:T(8,128)(2,1)}, bf16[32,128,256]{2,1,0:T(8,128)(2,1)}) async-done(((bf16[32,128,256]{2,1,0:T(8,128)(2,1)}, bf16[32,128,256]{2,1,0:T(8,128)(2,1)}), (bf16[32,128,256]{2,1,0:T(8,128)(2,1)}, bf16[32,128,256]{2,1,0:T(8,128)(2,1)})) %all-reduce.9.cloned.1.call-update) | async-done | bytes 4194320 | tf_op jit(solution)/shard_map/psum | solution.py:9
  111.1 4.4 %gather_fusion.1 = bf16[64,128,256]{2,1,0:T(8,128)(2,1)} fusion(bf16[32,128,256]{2,1,0:T(8,128)(2,1)} %get-tuple-element.34, s32[1024]{0:T(1024)S(1)} %get-tuple-element.56), kind=kCustom, calls=%fused_computation.1.clone | custom fusion | bytes 8388864 | tf_op jit(solution)/shard_map/jit(_take)/gather | solution.py:102
  115.5 6.3 %fusion.24 = bf16[64,256,128]{2,1,0:T(8,128)(2,1)} fusion(bf16[64,128,256]{2,1,0:T(8,128)(2,1)} %gather_fusion.1, pred[64]{0:T(512)(128)(4,1)S(1)} %get-tuple-element.48, bf16[1,2,64,128,128]{4,3,2,1,0:T(8,128)(2,1)} %param.17), kind=kOutput, calls=%fused_computation.42 | convolution fusion | flops 538968064 | bytes 10485824 | tf_op jit(solution)/shard_map/mab,mbf->maf/dot_general | solution.py:103
  121.8 6.9 %copy.29 = bf16[64,256,128]{1,0,2:T(8,128)(2,1)} copy(bf16[64,256,128]{2,1,0:T(8,128)(2,1)} %fusion.24) | data formatting | bytes 8388608 | tf_op jit(solution)/shard_map/mab,mbf->maf/dot_general | solution.py:103
  128.6 4.4 %gather_fusion = bf16[64,128,256]{2,1,0:T(8,128)(2,1)} fusion(bf16[32,128,256]{2,1,0:T(8,128)(2,1)} %get-tuple-element.35, s32[1024]{0:T(1024)S(1)} %get-tuple-element.57), kind=kCustom, calls=%fused_computation.clone | custom fusion | bytes 8388864 | tf_op jit(solution)/shard_map/jit(_take)/gather | solution.py:102
  133.0 6.3 %fusion.26 = bf16[64,256,128]{2,1,0:T(8,128)(2,1)} fusion(bf16[64,128,256]{2,1,0:T(8,128)(2,1)} %gather_fusion, pred[64]{0:T(512)(128)(4,1)S(1)} %get-tuple-element.38, bf16[1,2,64,128,128]{4,3,2,1,0:T(8,128)(2,1)} %param.17), kind=kOutput, calls=%fused_computation.44 | convolution fusion | flops 538968064 | bytes 10485824 | tf_op jit(solution)/shard_map/mab,mbf->maf/dot_general | solution.py:103
  139.3 6.8 %copy.28 = bf16[64,256,128]{1,0,2:T(8,128)(2,1)} copy(bf16[64,256,128]{2,1,0:T(8,128)(2,1)} %fusion.26) | data formatting | bytes 8388608 | tf_op jit(solution)/shard_map/mab,mbf->maf/dot_general | solution.py:103
  146.1 3.1 fusion
  149.2 0.4 copy-done.6
  149.6 0.7 fusion.32
  150.3 4.4 %copy.24 = f32[32,128,256]{2,1,0:T(8,128)} copy(f32[32,128,256]{2,0,1:T(8,128)S(1)} %fusion.32) | data formatting | bytes 8388608 | tf_op jit(solution)/shard_map/add | solution.py:110
  154.7 144.9 %all-reduce.10 = bf16[4096,256]{1,0:T(8,128)(2,1)} all-reduce(f32[4096,256]{1,0:T(8,128)} %bitcast.53), channel_id=1, replica_groups=mesh['blk'=8,'rep'=4] {'rep'}, use_global_device_ids=true, to_apply=%region_2.4 | all-reduce | flops 1048576 | bytes 6291456 | tf_op jit(solution)/shard_map/psum | solution.py:112
  299.5 0.0 copy-done.12
  299.5 0.0 copy-done.15
  299.5 2.4 fusion.5
  302.0 0.0 copy-done
  302.0 0.0 copy-done.14
  302.0 0.0 slice-start.1
  302.0 6.3 %convolution_add_fusion = f32[4096,768]{1,0:T(8,128)} fusion(bf16[256,768]{1,0:T(8,128)(2,1)S(1)} %copy-done, f32[768]{0:T(1024)S(1)} %copy-done.14, f32[4096,256]{1,0:T(8,128)S(1)} %fusion.5), kind=kOutput, calls=%fused_computation.6 | convolution fusion | flops 1614807040 | bytes 17173504 | tf_op jit(solution)/shard_map/dot_general | solution.py:30
  308.4 0.0 slice-done
  308.4 0.0 slice-done.1
  308.4 0.0 copy-start.13
  308.4 3.6 fusion.19
  312.0 0.0 copy-done.4
  312.0 0.0 copy-done.13
  312.0 0.0 copy-start.1
  312.0 9.2 %fusion.76 = (bf16[4096,256]{1,0:T(8,128)(2,1)}, f32[4096,256]{1,0:T(8,128)S(1)}, f32[4096,256]{1,0:T(8,128)}) fusion(bf16[4096,256]{1,0:T(8,128)(2,1)S(1)} %copy-done.3, bf16[4096,256]{1,0:T(8,128)(2,1)S(1)} %copy-done.4, f32[4096,512]{1,0:T(8,128)} %fusion.80, f32[4096,768]{1,0:T(8,128)} %convolution_add_fusion, bf16[256,256]{1,0:T(8,128)(2,1)S(1)} %copy-done.13, ...), kind=kOutput, calls=%fused_computation.103 | convolution fusion | flops 553648128 | bytes 33685504 | tf_op jit(solution)/shard_map/dot_general | solution.py:38
  321.2 5.0 %fusion.72 = bf16[4096,256]{1,0:T(8,128)(2,1)S(1)} fusion(f32[4096,256]{1,0:T(8,128)} %get-tuple-element.52, f32[4096,256]{1,0:T(8,128)S(1)} %get-tuple-element.37, bf16[4096,256]{1,0:T(8,128)(2,1)S(1)} %copy-done.4), kind=kLoop, calls=%fused_computation.101 | loop fusion | flops 7340032 | bytes 12582912 | tf_op jit(solution)/shard_map/convert_element_type | solution.py:44
  326.2 0.0 copy-start.7
  326.2 1.6 convolution_multiply_fusion.1
  327.8 0.6 copy-done.7
  328.5 4.9 %fusion.75 = (f32[256]{0:T(256)S(1)}, f32[256]{0:T(256)S(1)}, f32[256]{0:T(256)S(1)}, bf16[4096,256]{1,0:T(8,128)(2,1)S(1)}, bf16[4096,256]{1,0:T(8,128)(2,1)}, /*index=5*/f32[4096,256]{1,0:T(8,128)}) fusion(f32[4096,256]{1,0:T(8,128)S(1)} %get-tuple-element.37, f32[4096,256]{1,0:T(8,128)S(1)} %copy-done.7, bf16[4096,256]{1,0:T(8,128)(2,1)S(1)} %copy-done.3, ...), kind=kOutput, calls=%fused_computation.102 | convolution fusion | flops 560987392 | bytes 27397120 | tf_op jit(solution)/shard_map/dot_general | solution.py:19
  333.4 4.5 %fusion.45 = f32[256,512]{0,1:T(8,128)} fusion(bf16[4096,256]{1,0:T(8,128)(2,1)S(1)} %copy-done.3, bf16[4096,256]{1,0:T(8,128)(2,1)} %get-tuple-element.36, bf16[4096,256]{1,0:T(8,128)(2,1)S(1)} %get-tuple-element.42), kind=kOutput, calls=%fused_computation.63 | convolution fusion | flops 1082261504 | bytes 6815744 | tf_op jit(solution)/shard_map/dot_general | solution.py:13
  337.9 2.8 fusion.43
  340.7 2.7 fusion.79
  343.4 0.0 copy-start.5
  343.4 1.5 fusion.46
  344.9 0.0 all-reduce.7.cloned.1.call-update
  344.9 15.0 %all-reduce = (f32[256]{0:T(256)}, f32[768]{0:T(1024)}) all-reduce(f32[256]{0:T(256)S(1)} %broadcast_multiply_fusion, f32[768]{0:T(1024)S(1)} %maximum_multiply_fusion), channel_id=1, replica_groups=mesh['blk'=8,'rep'=4] {'blk'}, use_global_device_ids=true, to_apply=%region_5.7 | all-reduce | flops 1024 | bytes 8192 | tf_op jit(solution)/shard_map/psum | solution.py:117
  359.9 8.6 %fusion.6 = bf16[4096,256]{1,0:T(8,128)(2,1)} fusion(bf16[256,512]{1,0:T(8,128)(2,1)S(1)} %copy-done.11, f32[4096,256]{1,0:T(8,128)} %copy-done.2, bf16[4096,256]{1,0:T(8,128)(2,1)S(1)} %copy-done.5, f32[4096,256]{1,0:T(8,128)} %get-tuple-element.53, f32[4096,256]{1,0:T(8,128)} %copy-done.1, bf16[4096,256]{1,0:T(8,128)(2,1)} %get-tuple-element.36, ...), kind=kOutput, calls=%fused_computation.21 | convolution fusion | flops 1088421888 | bytes 21233664 | tf_op jit(solution)/shard_map/dot_general | solution.py:19
  368.5 39.8 %all-reduce.7.cloned.1.call-done = (f32[256,256]{1,0:T(8,128)}, f32[256,768]{1,0:T(8,128)}, f32[256,512]{0,1:T(8,128)}, f32[256,256]{1,0:T(8,128)}) async-done(((f32[256,256]{1,0:T(8,128)}, f32[256,768]{1,0:T(8,128)}, f32[256,512]{0,1:T(8,128)}, f32[256,256]{1,0:T(8,128)}), (f32[256,256]{1,0:T(8,128)}, f32[256,768]{1,0:T(8,128)}, f32[256,512]{0,1:T(8,128)}, ...) | async-done | bytes 1835024 | tf_op jit(solution)/shard_map/psum | solution.py:117
  408.2 2.0 copy.27
  410.3 1.7 copy.39
  411.9 2.1 copy.40
  414.0 1.7 copy.41
  (22 shorter events, 0.1 us)
Async XLA Ops:
  7.2 294.8 %copy-start = (bf16[256,768]{1,0:T(8,128)(2,1)S(1)}, bf16[256,768]{1,0:T(8,128)(2,1)}, u32[]{:S(2)}) copy-start(bf16[256,768]{1,0:T(8,128)(2,1)} %param.23) | copy-start | bytes 1179652
  7.2 103.9 %all-reduce.9.cloned.1.call-start = ((), (), s32[]{:S(2)}) async-start(), calls=%async_computation.1 | async-start | bytes 8388608 | tf_op jit(solution)/shard_map/psum | solution.py:9
  7.2 4.2 copy-start.16
  7.2 6.0 %copy-start.17 = (s32[1,2,64]{2,1,0:T(2,128)S(1)}, s32[1,2,64]{2,1,0:T(2,128)}, u32[]{:S(2)}) copy-start(s32[1,2,64]{2,1,0:T(2,128)} %param.20) | copy-start | bytes 1540
  7.3 6.1 %copy-start.18 = (s32[1,2,64]{2,1,0:T(2,128)S(1)}, s32[1,2,64]{2,1,0:T(2,128)}, u32[]{:S(2)}) copy-start(s32[1,2,64]{2,1,0:T(2,128)} %param.19) | copy-start | bytes 1540
  7.3 6.1 %copy-start.3 = (bf16[4096,256]{1,0:T(8,128)(2,1)S(1)}, bf16[4096,256]{1,0:T(8,128)(2,1)}, u32[]{:S(2)}) copy-start(bf16[4096,256]{1,0:T(8,128)(2,1)} %param.16) | copy-start | bytes 6291460
  7.3 6.1 %copy-start.11 = (bf16[256,512]{1,0:T(8,128)(2,1)S(1)}, bf16[256,512]{1,0:T(8,128)(2,1)}, u32[]{:S(2)}) copy-start(bf16[256,512]{1,0:T(8,128)(2,1)} %param.24) | copy-start | bytes 786436
  11.3 396.9 %all-reduce.7.cloned.1.call-start = ((), (), s32[]{:S(2)}) async-start(), calls=%async_computation | async-start | bytes 3670016 | tf_op jit(solution)/shard_map/psum | solution.py:117
  146.1 3.4 copy-start.6
  154.7 144.9 %copy-start.12 = (bf16[256,256]{1,0:T(8,128)(2,1)S(1)}, bf16[256,256]{1,0:T(8,128)(2,1)}, u32[]{:S(2)}) copy-start(bf16[256,256]{1,0:T(8,128)(2,1)} %param.21) | copy-start | bytes 393220
  154.7 144.9 %copy-start.15 = (f32[256]{0:T(256)S(1)}, f32[256]{0:T(256)}, u32[]{:S(2)}) copy-start(f32[256]{0:T(256)} %param.22) | copy-start | bytes 3076
  299.5 2.5 copy-start.14
  299.5 8.8 %slice-start = ((s8[8388608]{0:T(1024)(128)(4,1)}), s8[4194304]{0:T(1024)(128)(4,1)S(1)}, s32[]{:S(2)}) async-start(s8[8388608]{0:T(1024)(128)(4,1)} %bitcast.51), calls=%async_computation.2 | async-start | bytes 8388608
  302.0 6.4 %slice-start.1 = ((s8[8388608]{0:T(1024)(128)(4,1)}), s8[4194304]{0:T(1024)(128)(4,1)S(1)}, s32[]{:S(2)}) async-start(s8[8388608]{0:T(1024)(128)(4,1)} %bitcast.51), calls=%async_computation.3 | async-start | bytes 8388608
  308.4 3.6 copy-start.4
  308.4 3.6 copy-start.13
  312.0 15.8 %copy-start.1 = (f32[4096,256]{1,0:T(8,128)}, f32[4096,256]{1,0:T(8,128)S(1)}, u32[]{:S(2)}) copy-start(f32[4096,256]{1,0:T(8,128)S(1)} %fusion.19) | copy-start | bytes 12582916
  321.2 6.6 %copy-start.2 = (f32[4096,256]{1,0:T(8,128)}, f32[4096,256]{1,0:T(8,128)S(1)}, u32[]{:S(2)}) copy-start(f32[4096,256]{1,0:T(8,128)S(1)} %get-tuple-element.37) | copy-start | bytes 12582916
  326.2 2.3 copy-start.7
  333.4 7.2 %copy-start.9 = (bf16[4096,256]{1,0:T(8,128)(2,1)}, bf16[4096,256]{1,0:T(8,128)(2,1)S(1)}, u32[]{:S(2)}) copy-start(bf16[4096,256]{1,0:T(8,128)(2,1)S(1)} %get-tuple-element.42) | copy-start | bytes 6291460
  333.4 4.5 %copy-start.10 = (bf16[4096,256]{1,0:T(8,128)(2,1)S(1)}, bf16[4096,256]{1,0:T(8,128)(2,1)}, u32[]{:S(2)}) copy-start(bf16[4096,256]{1,0:T(8,128)(2,1)} %get-tuple-element.36) | copy-start | bytes 6291460
  340.7 2.7 copy-start.8
  343.4 16.5 %copy-start.5 = (bf16[4096,256]{1,0:T(8,128)(2,1)S(1)}, bf16[4096,256]{1,0:T(8,128)(2,1)}, u32[]{:S(2)}) copy-start(bf16[4096,256]{1,0:T(8,128)(2,1)} %param.27) | copy-start | bytes 6291460
Sparse Core Ops, SparseCore 0:
  11.5 99.6 all-reduce.8
  345.0 63.1 all-reduce.6
where the time goes:
time: 423 us
  blocking collectives  160 us (38%)
  waiting for transfers between devices  133 us (31%)
  matrix products  65.4 us (15%)
  local copies, waits for them, and re-layouts  35.9 us (8%)
  between operations  14.3 us (3%)
  other arithmetic  13.9 us (3%)
    psum x1, blocking collectives, local(): totals = lax.psum(flat, 'rep')  145 us
    psum x1, waiting for transfers between devices, from_root(): return lax.psum(block, axis)  93.3 us
    psum x1, waiting for transfers between devices, local(): lax.psum((grad_graph * scale, graph_bias_sum * scale, grad_input * scale,...  39.8 us
    dot_general x3, matrix products, contract_last(): lax.dot_general(left, right, (((1,), (1,)), ((), ())), preferred_element_...  16.2 us
    psum x1, blocking collectives, local(): lax.psum((grad_graph * scale, graph_bias_sum * scale, grad_input * scale,...  15 us
    dot_general x2, local copies, waits for them, and re-layouts, local(): jnp.einsum('mab,mbf->maf', tiles[0, slot], picked, preferred_element_type...  13.7 us
    dot_general x2, matrix products, local(): jnp.einsum('mab,mbf->maf', tiles[0, slot], picked, preferred_element_type...  12.6 us
    dot_general x4, matrix products, contract_first(): lax.dot_general(left, right, (((0,), (0,)), ((), ())), preferred_element_...  10.3 us
  transfers between devices with their start and end apart: 2, of which 2 were waited for; matrix products, arithmetic and copies ran while one was open for 4% of the time, Pallas kernels for 0%

commit v1 on v0

v1 whole, which is shorter than its diff:
```python
import functools

import jax
import jax.numpy as jnp
from jax import lax
from jax.experimental import pallas as pl
from jax.experimental.pallas import tpu as pltpu
from jax.sharding import PartitionSpec as P

MESH = pl.DeviceIdType.MESH
CHUNKS = 32
WINDOW = 4
GROUP = 8
ROW_BLOCK = 256
VMEM_LIMIT = 56 * 1024 * 1024


def contract_first(left, right):
    return lax.dot_general(
        left, right, (((0,), (0,)), ((), ())), preferred_element_type=jnp.float32
    )


def contract_last(left, right):
    return lax.dot_general(
        left, right, (((1,), (1,)), ((), ())), preferred_element_type=jnp.float32
    )


def product(left, right):
    return jnp.dot(left, right, preferred_element_type=jnp.float32)


def spread_kernel(chips, feat, out, up_sem, down_sem, recv_sem, pair_sem, pair_recv, own_sem):
    blk = lax.axis_index("blk")
    rep = lax.axis_index("rep")
    core = blk % 2
    chip = blk // 2
    above = (chip + 1) % chips
    below = (chip + chips - 1) % chips
    chunk = feat.shape[0] // CHUNKS

    barrier = pltpu.get_barrier_semaphore()
    for other in (above * 2 + core, below * 2 + core, chip * 2 + 1 - core):
        pl.semaphore_signal(
            barrier, inc=1, device_id={"blk": other, "rep": rep}, device_id_type=MESH
        )
    pl.semaphore_wait(barrier, 3)

    def rows_of(j):
        return pl.ds(pl.multiple_of(j * chunk, chunk), chunk)

    def send(src, j, target, send_sem, recv):
        return pltpu.make_async_remote_copy(
            src_ref=src,
            dst_ref=out.at[core, rows_of(j)],
            send_sem=send_sem.at[j],
            recv_sem=recv.at[j],
            device_id={"blk": target, "rep": rep},
            device_id_type=MESH,
        )

    def up(src, j):
        return send(src, j, above * 2 + core, up_sem, recv_sem)

    def down(src, j):
        return send(src, j, below * 2 + core, down_sem, recv_sem)

    def pair(src, j):
        return send(src, j, chip * 2 + 1 - core, pair_sem, pair_recv)

    has_up = jnp.logical_and(chip >= rep, chip < chips - 1)
    has_down = jnp.logical_and(chip <= rep, chip > 0)
    is_owner = chip == rep

    @pl.when(is_owner)
    def _():
        own = pltpu.make_async_copy(feat, out.at[core], own_sem)
        own.start()

        def step(j, carry):
            src = feat.at[rows_of(j)]

            @pl.when(has_up)
            def _():
                @pl.when(j >= WINDOW)
                def _():
                    up(feat.at[rows_of(j - WINDOW)], j - WINDOW).wait_send()

                up(src, j).start()

            @pl.when(has_down)
            def _():
                @pl.when(j >= WINDOW)
                def _():
                    down(feat.at[rows_of(j - WINDOW)], j - WINDOW).wait_send()

                down(src, j).start()

            pair(src, j).start()
            return carry

        lax.fori_loop(0, CHUNKS, step, 0)

        def finish(j, carry):
            src = feat.at[rows_of(j)]

            @pl.when(jnp.logical_and(has_up, j >= CHUNKS - WINDOW))
            def _():
                up(src, j).wait_send()

            @pl.when(jnp.logical_and(has_down, j >= CHUNKS - WINDOW))
            def _():
                down(src, j).wait_send()

            pair(src, j).wait()
            return carry

        lax.fori_loop(0, CHUNKS, finish, 0)
        own.wait()

    @pl.when(jnp.logical_not(is_owner))
    def _():
        def step(j, carry):
            src = out.at[core, rows_of(j)]
            up(src, j).wait_recv()

            @pl.when(has_up)
            def _():
                up(src, j).start()

            @pl.when(has_down)
            def _():
                down(src, j).start()

            pair(src, j).start()
            return carry

        lax.fori_loop(0, CHUNKS, step, 0)

        def finish(j, carry):
            src = out.at[core, rows_of(j)]

            @pl.when(has_up)
            def _():
                up(src, j).wait_send()

            @pl.when(has_down)
            def _():
                down(src, j).wait_send()

            pair(src, j).wait()
            return carry

        lax.fori_loop(0, CHUNKS, finish, 0)


def spread(features, chips, per_rep):
    dma = pltpu.SemaphoreType.DMA((CHUNKS,))
    return pl.pallas_call(
        functools.partial(spread_kernel, chips),
        out_shape=jax.ShapeDtypeStruct((per_rep,) + features.shape, features.dtype),
        in_specs=[pl.BlockSpec(memory_space=pl.ANY)],
        out_specs=pl.BlockSpec(memory_space=pl.ANY),
        scratch_shapes=[dma, dma, dma, dma, dma, pltpu.SemaphoreType.DMA(())],
        compiler_params=pltpu.CompilerParams(
            collective_id=0, has_side_effects=True, vmem_limit_bytes=VMEM_LIMIT
        ),
    )(features)


def tiles_kernel(count, rows, cols, tiles, sections, out, acc):
    slot = pl.program_id(0)
    side = tiles.shape[2]

    @pl.when(slot == 0)
    def _():
        acc[...] = jnp.zeros_like(acc)

    used = count[0, slot]

    def step(g, carry):
        terms = []
        for i in range(GROUP):
            m = g * GROUP + i
            col = pl.multiple_of(cols[0, slot, m] * side, side)
            term = product(tiles[0, m], sections[0, pl.ds(col, side), :])
            terms.append(jnp.where(m < used, term, 0.0))
        for i in range(GROUP):
            row = pl.multiple_of(rows[0, slot, g * GROUP + i] * side, side)
            acc[pl.ds(row, side), :] += terms[i]
        return carry

    lax.fori_loop(0, (used + GROUP - 1) // GROUP, step, 0)

    @pl.when(slot == pl.num_programs(0) - 1)
    def _():
        out[...] = acc[...].astype(out.dtype)


def tile_products(count, rows, cols, tiles, sections):
    per_rep, cap, side = tiles.shape[:3]
    node_rows, width = sections.shape[1:]
    return pl.pallas_call(
        tiles_kernel,
        out_shape=jax.ShapeDtypeStruct((node_rows, width), jnp.bfloat16),
        grid_spec=pltpu.PrefetchScalarGridSpec(
            num_scalar_prefetch=3,
            grid=(per_rep,),
            in_specs=[
                pl.BlockSpec((1, cap, side, side), lambda s, *_: (s, 0, 0, 0)),
                pl.BlockSpec((1, node_rows, width), lambda s, *_: (s, 0, 0)),
            ],
            out_specs=pl.BlockSpec((node_rows, width), lambda s, *_: (0, 0)),
            scratch_shapes=[pltpu.VMEM((node_rows, width), jnp.float32)],
        ),
        compiler_params=pltpu.CompilerParams(vmem_limit_bytes=VMEM_LIMIT),
    )(count, rows, cols, tiles, sections)


def cell_kernel(
    chips,
    reps,
    scale,
    partial,
    state_hbm,
    cot_hbm,
    w_graph,
    b_graph,
    w_input,
    w_state,
    w_cand,
    b_gates,
    new_state,
    state_grad,
    grad_graph,
    graph_bias,
    grad_input,
    grad_state,
    grad_cand,
    gate_sums,
    state_v,
    cot_v,
    s_all,
    part_own,
    part_recv,
    grads,
    grads_b,
    half_recv,
    half_b,
    chip_recv,
    rep_recv,
    final,
    local_sem,
    rs_send,
    rs_recv,
    ag_send,
    ag_recv,
    pair_send,
    pair_recv,
    chip_send,
    chip_got,
    rep_send,
    rep_got,
    chip_send2,
    chip_got2,
):
    blk = lax.axis_index("blk")
    rep = lax.axis_index("rep")
    core = blk % 2
    chip = blk // 2
    width = w_cand.shape[0]
    part_rows = partial.shape[0] // reps
    half_rows = half_b.shape[0]
    piece_rows = rep_recv.shape[1]
    weight_rows = 7 * width

    def rep_at(k):
        return ((rep // 2 + k // 2) % (reps // 2)) * 2 + (rep % 2 + k % 2) % 2

    def rep_from(k):
        return ((rep // 2 + reps // 2 - k // 2) % (reps // 2)) * 2 + (rep % 2 + k % 2) % 2

    def on_rep(k):
        return {"blk": blk, "rep": rep_at(k)}

    def chip_at(k):
        return (chip + k) % chips

    def on_chip(k):
        return {"blk": chip_at(k) * 2 + core, "rep": rep}

    mate = {"blk": chip * 2 + 1 - core, "rep": rep}

    def part(index):
        return pl.ds(pl.multiple_of(index * part_rows, part_rows), part_rows)

    def piece(index):
        return pl.ds(pl.multiple_of(index * piece_rows, piece_rows), piece_rows)

    def half(index):
        return pl.ds(pl.multiple_of(index * half_rows, half_rows), half_rows)

    def remote(src, dst, send_sem, recv_sem, target):
        return pltpu.make_async_remote_copy(
            src_ref=src,
            dst_ref=dst,
            send_sem=send_sem,
            recv_sem=recv_sem,
            device_id=target,
            device_id_type=MESH,
        )

    loads = [
        pltpu.make_async_copy(partial.at[part(rep)], part_own, local_sem.at[0]),
        pltpu.make_async_copy(state_hbm, state_v, local_sem.at[1]),
        pltpu.make_async_copy(cot_hbm, cot_v, local_sem.at[2]),
    ]
    for load in loads:
        load.start()

    barrier = pltpu.get_barrier_semaphore()
    targets = [on_rep(k) for k in range(1, reps)] + [on_chip(k) for k in range(1, chips)] + [mate]
    for target in targets:
        pl.semaphore_signal(barrier, inc=1, device_id=target, device_id_type=MESH)
    pl.semaphore_wait(barrier, len(targets))

    scatter = [
        remote(
            partial.at[part(rep_at(k))],
            part_recv.at[k - 1],
            rs_send.at[k - 1],
            rs_recv.at[k - 1],
            on_rep(k),
        )
        for k in range(1, reps)
    ]
    for copy in reversed(scatter):
        copy.start()
    grads[...] = jnp.zeros_like(grads)
    for load in loads:
        load.wait()
    for copy in scatter:
        copy.wait()

    own_base = rep * part_rows

    def add_up(i, carry):
        here = pl.ds(pl.multiple_of(i * ROW_BLOCK, ROW_BLOCK), ROW_BLOCK)
        total = part_own[here, :].astype(jnp.float32)
        for k in range(reps - 1):
            total = total + part_recv[k, here, :].astype(jnp.float32)
        there = pl.ds(pl.multiple_of(own_base + i * ROW_BLOCK, ROW_BLOCK), ROW_BLOCK)
        s_all[there, :] = total.astype(jnp.bfloat16)
        return carry

    lax.fori_loop(0, part_rows // ROW_BLOCK, add_up, 0)

    gather = [
        remote(
            s_all.at[part(rep)],
            s_all.at[part(rep)],
            ag_send.at[k - 1],
            ag_recv.at[k - 1],
            on_rep(k),
        )
        for k in range(1, reps)
    ]
    for copy in gather:
        copy.start()

    def cell(base, with_grads):
        def step(i, carry):
            here = pl.ds(pl.multiple_of(base + i * ROW_BLOCK, ROW_BLOCK), ROW_BLOCK)
            summed_b = s_all[here, :]
            state = state_v[here, :]
            graph_out = jnp.tanh(product(summed_b, w_graph[...]) + b_graph[...])
            graph_b = graph_out.astype(jnp.bfloat16)
            from_input = product(graph_b, w_input[...]) + b_gates[...]
            from_state = product(state, w_state[...])
            reset_gate = jax.nn.sigmoid(from_input[:, :width] + from_state[:, :width])
            update_gate = jax.nn.sigmoid(from_input[:, width : 2 * width] + from_state[:, width:])
            state_f = state.astype(jnp.float32)
            reset_state = (reset_gate * state_f).astype(jnp.bfloat16)
            candidate = jnp.tanh(from_input[:, 2 * width :] + product(reset_state, w_cand[...]))
            keep = 1.0 - update_gate
            new_state[here, :] = (update_gate * state_f + keep * candidate).astype(jnp.bfloat16)
            upstream = cot_v[here, :].astype(jnp.float32)
            grad_update = upstream * (state_f - candidate) * update_gate * keep
            grad_cand_f = upstream * keep * (1.0 - candidate * candidate)
            grad_cand_b = grad_cand_f.astype(jnp.bfloat16)
            grad_reset_state = contract_last(grad_cand_b, w_cand[...])
            grad_reset = grad_reset_state * state_f * reset_gate * (1.0 - reset_gate)
            gates_b = jnp.concatenate(
                [grad_reset.astype(jnp.bfloat16), grad_update.astype(jnp.bfloat16)], axis=1
            )
            state_grad[here, :] = (
                upstream * update_gate
                + grad_reset_state * reset_gate
                + contract_last(gates_b, w_state[...])
            ).astype(jnp.bfloat16)
            if with_grads:
                all_b = jnp.concatenate([gates_b, grad_cand_b], axis=1)
                grad_preact = contract_last(all_b, w_input[...]) * (1.0 - graph_out * graph_out)

                def add(at, value):
                    rows = pl.ds(at, value.shape[0])
                    grads[rows, :] += value

                add(0, contract_first(summed_b, grad_preact.astype(jnp.bfloat16)))
                to_input = contract_first(graph_b, all_b)
                for n in range(3):
                    add((1 + n) * width, to_input[:, n * width : (n + 1) * width])
                to_state = contract_first(state, gates_b)
                for n in range(2):
                    add((4 + n) * width, to_state[:, n * width : (n + 1) * width])
                add(6 * width, contract_first(reset_state, grad_cand_b))
                sums = [
                    jnp.sum(term, axis=0, keepdims=True)
                    for term in (grad_preact, grad_reset, grad_update, grad_cand_f)
                ]
                add(weight_rows, jnp.concatenate(sums + [jnp.zeros((4, width), jnp.float32)]))
            return carry

        lax.fori_loop(0, part_rows // ROW_BLOCK, step, 0)

    cell(own_base, True)

    to_mate = remote(
        grads_b.at[half(1 - core)], half_recv, pair_send.at[0], pair_recv.at[0], mate
    )
    between = [
        remote(
            half_b.at[piece(chip_at(k))],
            chip_recv.at[k - 1],
            chip_send.at[k - 1],
            chip_got.at[k - 1],
            on_chip(k),
        )
        for k in range(1, chips)
    ]
    across = [
        remote(
            rep_recv.at[rep], rep_recv.at[rep], rep_send.at[k - 1], rep_got.at[k - 1], on_rep(k)
        )
        for k in range(1, reps)
    ]
    mine = piece(core * chips + chip)
    back = [
        remote(
            final.at[mine], final.at[mine], chip_send2.at[k - 1], chip_got2.at[k - 1], on_chip(k)
        )
        for k in range(1, chips)
    ]
    back_mate = remote(
        final.at[half(core)], final.at[half(core)], pair_send.at[1], pair_recv.at[1], mate
    )

    def stage_pair():
        to_mate.wait()
        half_b[...] = (grads[half(core), :] + half_recv[...].astype(jnp.float32)).astype(
            jnp.bfloat16
        )
        for copy in between:
            copy.start()

    def stage_chip():
        for copy in between:
            copy.wait()
        total = half_b[piece(chip), :].astype(jnp.float32)
        for k in range(chips - 1):
            total = total + chip_recv[k].astype(jnp.float32)
        rep_recv[rep] = total.astype(jnp.bfloat16)
        for copy in across:
            copy.start()

    def stage_rep():
        for copy in across:
            copy.wait()
        total = rep_recv[0].astype(jnp.float32)
        for k in range(1, reps):
            total = total + rep_recv[k].astype(jnp.float32)
        final[mine, :] = (total * scale).astype(jnp.bfloat16)
        for copy in back:
            copy.start()

    def stage_back():
        for copy in back:
            copy.wait()
        back_mate.start()

    grads_b[...] = grads[...].astype(jnp.bfloat16)
    to_mate.start()
    stages = [stage_pair, stage_chip, stage_rep, stage_back]
    for k in range(1, reps):
        gather[k - 1].wait()
        cell(rep_from(k) * part_rows, False)
        if stages:
            stages.pop(0)()
    for stage in stages:
        stage()
    back_mate.wait()

    def take(at, count):
        return final[pl.ds(at, count), :].astype(jnp.float32)

    grad_graph[...] = take(0, width)
    for n in range(3):
        grad_input[:, n * width : (n + 1) * width] = take((1 + n) * width, width)
    for n in range(2):
        grad_state[:, n * width : (n + 1) * width] = take((4 + n) * width, width)
    grad_cand[...] = take(6 * width, width)
    bias = take(weight_rows, 16)
    graph_bias[...] = bias[0:1]
    for n in range(3):
        gate_sums[:, n * width : (n + 1) * width] = bias[1 + n : 2 + n]


def cell_step(partial, state, cotangent, weights, chips, reps):
    node_rows, width = partial.shape
    blks = chips * 2
    unit = 16 * blks
    grad_rows = (7 * width + 16 + unit - 1) // unit * unit
    half_rows = grad_rows // 2
    piece_rows = grad_rows // blks
    part_rows = node_rows // reps
    scale = float(node_rows * blks) ** (-0.5)
    f32, b16 = jnp.float32, jnp.bfloat16
    shape = jax.ShapeDtypeStruct
    whole = pl.BlockSpec(memory_space=pltpu.VMEM)
    anywhere = pl.BlockSpec(memory_space=pl.ANY)
    dma = pltpu.SemaphoreType.DMA
    return pl.pallas_call(
        functools.partial(cell_kernel, chips, reps, scale),
        out_shape=[
            shape((node_rows, width), b16),
            shape((node_rows, width), b16),
            shape((width, width), f32),
            shape((1, width), f32),
            shape((width, 3 * width), f32),
            shape((width, 2 * width), f32),
            shape((width, width), f32),
            shape((1, 3 * width), f32),
        ],
        in_specs=[anywhere] * 3 + [whole] * 6,
        out_specs=[whole] * 8,
        scratch_shapes=[
            pltpu.VMEM((node_rows, width), b16),
            pltpu.VMEM((node_rows, width), b16),
            pltpu.VMEM((node_rows, width), b16),
            pltpu.VMEM((part_rows, width), b16),
            pltpu.VMEM((reps - 1, part_rows, width), b16),
            pltpu.VMEM((grad_rows, width), f32),
            pltpu.VMEM((grad_rows, width), b16),
            pltpu.VMEM((half_rows, width), b16),
            pltpu.VMEM((half_rows, width), b16),
            pltpu.VMEM((chips - 1, piece_rows, width), b16),
            pltpu.VMEM((reps, piece_rows, width), b16),
            pltpu.VMEM((grad_rows, width), b16),
            dma((3,)),
            dma((reps - 1,)),
            dma((reps - 1,)),
            dma((reps - 1,)),
            dma((reps - 1,)),
            dma((2,)),
            dma((2,)),
            dma((chips - 1,)),
            dma((chips - 1,)),
            dma((reps - 1,)),
            dma((reps - 1,)),
            dma((chips - 1,)),
            dma((chips - 1,)),
        ],
        compiler_params=pltpu.CompilerParams(
            collective_id=1, has_side_effects=True, vmem_limit_bytes=VMEM_LIMIT
        ),
    )(partial, state, cotangent, *weights)


def solution(mesh):
    chips = mesh.shape["blk"] // 2
    reps = mesh.shape["rep"]

    def local(
        features,
        state,
        tiles,
        tile_count,
        tile_rows,
        tile_cols,
        w_graph,
        b_graph,
        w_input,
        w_state,
        w_cand,
        b_gates,
        cotangent,
    ):
        sections = spread(features, chips, tiles.shape[1])
        partial = tile_products(tile_count, tile_rows, tile_cols, tiles[0], sections)
        weights = (
            w_graph,
            b_graph.reshape(1, -1),
            w_input,
            w_state,
            w_cand,
            b_gates.reshape(1, -1),
        )
        outs = cell_step(partial, state, cotangent, weights, chips, reps)
        return (
            outs[0],
            outs[1],
            outs[2],
            outs[3].reshape(-1),
            outs[4],
            outs[5],
            outs[6],
            outs[7].reshape(-1),
        )

    in_specs = (
        P("blk", None),
        P("blk", None),
        P("blk", "rep", None, None, None),
        P("blk", "rep"),
        P("blk", "rep", None),
        P("blk", "rep", None),
        P(),
        P(),
        P(),
        P(),
        P(),
        P(),
        P("blk", None),
    )
    out_specs = (P("blk", None), P("blk", None), P(), P(), P(), P(), P(), P())
    return jax.shard_map(local, mesh=mesh, in_specs=in_specs, out_specs=out_specs, check_vma=False)
```

time: 423 us -> 167 us (0.39)
  blocking collectives: 160 us -> 0 us
  Pallas kernels: 0 us -> 154 us
  waiting for transfers between devices: 133 us -> 0 us
  matrix products: 65.4 us -> 0 us
  local copies, waits for them, and re-layouts: 35.9 us -> 9.45 us
  between operations: 14.3 us -> 0.66 us
  other arithmetic: 13.9 us -> 1.29 us
    psum x2 -> x0, blocking collectives: 160 us -> none  [the longest x1 145 us: local(): totals = lax.psum(flat, 'rep')]
    pallas_call x0 -> x3, Pallas kernels: none -> 154 us  [the longest x1 74.9 us: cell_step(): pl.pallas_call(functools.partial(cell_kernel, chips, reps, scale), out_sh...]
    psum x2 -> x0, waiting for transfers between devices: 133 us -> none  [the longest x1 93.3 us: from_root(): return lax.psum(block, axis)]
    dot_general x15 -> x0, matrix products: 65.4 us -> none  [the longest x3 16.2 us: contract_last(): lax.dot_general(left, right, (((1,), (1,)), ((), ())), preferred_element_...]
    dot_general x2 -> x0, local copies, waits for them, and re-layouts: 13.7 us -> none  [local(): jnp.einsum('mab,mbf->maf', tiles[0, slot], picked, preferred_element_type...]
    gather x2 -> x0, local copies, waits for them, and re-layouts: 8.75 us -> none  [local(): picked = jnp.take(section_tiles, tile_cols[0, slot], axis=0)]
    convert_element_type x1 -> x0, other arithmetic: 4.97 us -> none  [cell_step(): grad_cand_b = grad_cand_f.astype(jnp.bfloat16)]
    add x1 -> x0, local copies, waits for them, and re-layouts: 4.39 us -> none  [local(): partial_value = partial_value + jnp.einsum('rm,maf->raf', placing, products)]
  transfers between devices with their start and end apart: 2 -> 0, of which waited for: 2 -> 0; matrix products, arithmetic and copies ran while one was open for 4% -> 0% of each run, Pallas kernels for 0% -> 0%
where the time goes in v1:
time: 167 us; the launch traced here: 166 us
  Pallas kernels  154 us (92%)
  local copies, waits for them, and re-layouts  9.45 us (6%)
    pallas_call x1, Pallas kernels, cell_step(): pl.pallas_call(functools.partial(cell_kernel, chips, reps, scale), out_sh...  74.9 us
    pallas_call x1, Pallas kernels, spread(): pl.pallas_call(functools.partial(spread_kernel, chips), out_shape=jax.Sha...  71.1 us
    unnamed x19, local copies, waits for them, and re-layouts  8.18 us
    pallas_call x1, Pallas kernels, tile_products(): pl.pallas_call(tiles_kernel, out_shape=jax.ShapeDtypeStruct((node_rows, w...  8.17 us

profile of v1, /device:TPU:0, one launch (start us, length us, event | category | flops | bytes accessed | tf_op | source)
XLA Modules:
  0.0 165.6 jit_solution(15940893855777112879)
XLA Ops:
  0.6 1.3 reshape.29.b_gates
  1.9 71.1 %shard_map.188.sections = bf16[2,4096,256]{2,1,0:T(8,128)(2,1)} custom-call(bf16[4096,256]{1,0:T(8,128)(2,1)} %feat.1), custom_call_target="tpu_custom_call" | custom-call | tf_op jit(solution)/shard_map/pallas_call | solution.py:160
  73.0 8.2 %shard_map.189.partial = bf16[4096,256]{1,0:T(8,128)(2,1)} custom-call(s32[1,2]{1,0:T(1,128)} %count.1, s32[1,2,64]{2,1,0:T(2,128)} %rows.1, s32[1,2,64]{2,1,0:T(2,128)} %cols.1, bf16[2,64,128,128]{3,2,1,0:T(8,128)(2,1)} %bitcast.3, bf16[2,4096,256]{2,1,0:T(8,128)(2,1)} %shard_map.188.sections), custom_call_target="tpu_custom_call" | custom-call | tf_op jit(solution)/shard_map/pallas_call | solution.py:204
  81.2 74.9 %shard_map.190 = (bf16[4096,256]{1,0:T(8,128)(2,1)}, bf16[4096,256]{1,0:T(8,128)(2,1)}, f32[256,256]{1,0:T(8,128)}, f32[1,256]{1,0:T(1,128)}, f32[256,768]{1,0:T...) custom-call(bf16[4096,256]{1,0:T(8,128)(2,1)} %shard_map.189.partial, ...), custom_call_target="tpu_custom_call" | custom-call | tf_op jit(solution)/shard_map/pallas_call | solution.py:533
  156.1 1.3 reduce
  157.4 0.0 copy-start
  157.4 3.2 %copy.28 = bf16[4096,256]{1,0:T(8,128)(2,1)} copy(bf16[4096,256]{1,0:T(8,128)(2,1)} %get-tuple-element.32) | data formatting | bytes 4194304
  160.6 0.0 copy-done
  160.6 0.0 copy-start.4
  160.6 0.0 copy-start.5
  160.6 0.0 copy-start.1
  160.6 1.3 copy.29
  161.9 0.0 copy-done.4
  161.9 0.0 copy-start.2
  161.9 0.0 copy-start.3
  161.9 0.7 copy.30
  162.6 0.0 copy-done.5
  162.6 0.6 copy.31
  163.2 0.0 copy-done.1
  163.2 0.9 copy.32
  164.0 0.0 copy-done.2
  164.1 0.8 copy.33
  164.8 0.0 copy-done.3
  164.8 0.7 copy.34
Async XLA Ops:
  157.4 3.2 %copy-start = (bf16[4096,256]{1,0:T(8,128)(2,1)S(1)}, bf16[4096,256]{1,0:T(8,128)(2,1)}, u32[]{:S(2)}) copy-start(bf16[4096,256]{1,0:T(8,128)(2,1)} %get-tuple-element.33) | copy-start | bytes 6291460
  160.6 1.3 copy-start.4
  160.6 2.0 %copy-start.5 = (f32[1,256]{1,0:T(1,128)S(1)}, f32[1,256]{1,0:T(1,128)}, u32[]{:S(2)}) copy-start(f32[1,256]{1,0:T(1,128)} %get-tuple-element.19) | copy-start | bytes 3076
  160.6 2.6 %copy-start.1 = (f32[256,768]{1,0:T(8,128)S(1)}, f32[256,768]{1,0:T(8,128)}, u32[]{:S(2)}) copy-start(f32[256,768]{1,0:T(8,128)} %get-tuple-element.36) | copy-start | bytes 2359300
  161.9 2.2 %copy-start.2 = (f32[256,512]{1,0:T(8,128)S(1)}, f32[256,512]{1,0:T(8,128)}, u32[]{:S(2)}) copy-start(f32[256,512]{1,0:T(8,128)} %get-tuple-element.37) | copy-start | bytes 1572868
  161.9 3.0 %copy-start.3 = (f32[256,256]{1,0:T(8,128)S(1)}, f32[256,256]{1,0:T(8,128)}, u32[]{:S(2)}) copy-start(f32[256,256]{1,0:T(8,128)} %get-tuple-element.38) | copy-start | bytes 786436
